TPU v7x, 512 devices: a whole 4x8x8 slice. The times are simulated.
512 devices in a mesh: dp: 32 (over x, z), resp: 16 (over y, core).
Axes of the slice: x: 4, y: 8, z: 8, core: 2. Of those that a mesh axis runs over, the one named last changes fastest.
Arguments:
- queries: bfloat16 [65536, 2560], P(('dp', 'resp')), parts along dimension 0, may hold values from -5 to 5
- keys: bfloat16 [65536, 2560], P(('dp', 'resp')), parts along dimension 0, may hold values from -5 to 5
- values: bfloat16 [65536, 2560], P(('dp', 'resp')), parts along dimension 0, may hold values from -6 to 6
- cotangent: bfloat16 [65536, 2560], P(('dp', 'resp')), parts along dimension 0, may hold values from -6 to 6
- lengths: int32 [512, 4], P(('dp', 'resp')), parts along dimension 0, may hold values from 0 to 32, as said below
- prompt_keys: bfloat16 [4096, 2560], P(('dp', 'resp')), parts along dimension 0, may hold values from -5 to 5
- prompt_values: bfloat16 [4096, 2560], P(('dp', 'resp')), parts along dimension 0, may hold values from -6 to 6
Outputs:
- query_grad: bfloat16 [65536, 2560], P(('dp', 'resp')), parts along dimension 0
- key_grad: bfloat16 [65536, 2560], P(('dp', 'resp')), parts along dimension 0
- value_grad: bfloat16 [65536, 2560], P(('dp', 'resp')), parts along dimension 0
- prompt_key_grad: bfloat16 [4096, 2560], P(('dp', 'resp')), parts along dimension 0
- prompt_value_grad: bfloat16 [4096, 2560], P(('dp', 'resp')), parts along dimension 0
There are 32 independent parts, one for each index of `dp`. A program takes and returns all parts, laid end to end along the dimension named above; each array names one. Nothing has to cross between parts.
Inputs may be any that keep to these rules, and one draw needn't show every extreme that they name: `lengths`: each row sums to at most 128; in every draw some row sums to exactly 128; a 0 means no response.
All inputs are finite; a program needn't handle non-finite values.
Results may differ from a plain program's by a relative error of at most 0.035.
Values may be sent and summed in bfloat16 or wider, within the bound.
A program may use at most 64 MiB of HBM per device.

v0:
```python
import jax
import jax.numpy as jnp
from jax import lax
from jax.sharding import PartitionSpec as P

HD = 128


def slot_layout(length_row, slots):
    ends = jnp.cumsum(length_row)
    place = jnp.arange(slots, dtype=jnp.int32)
    segment = jnp.sum((place[:, None] >= ends[None, :]).astype(jnp.int32), axis=1)
    live = place < ends[-1]
    return (place, segment, live)


def split_heads(block):
    return block.reshape(block.shape[0], block.shape[1] // HD, HD)


def scores_of(query3, key_block):
    return jnp.einsum(
        "qhd,khd->hqk", query3, split_heads(key_block), preferred_element_type=jnp.float32
    ) * HD ** (-0.5)


def per_device(queries, keys, values, cotangent, lengths, prompt_keys, prompt_values):
    slots, width = queries.shape
    scale = HD ** (-0.5)
    place, segment, live = slot_layout(lengths[0], slots)
    allowed_self = (
        (segment[:, None] == segment[None, :])
        & (place[None, :] <= place[:, None])
        & live[:, None]
        & live[None, :]
    )
    rowlive = live[None, :, None]
    query3 = split_heads(queries)
    cot3 = split_heads(cotangent)
    whole_keys, whole_values = (
        lax.all_gather(prompt_keys, "resp", axis=0, tiled=True),
        lax.all_gather(prompt_values, "resp", axis=0, tiled=True),
    )
    prompt_rows = whole_keys.shape[0]
    scores = jnp.concatenate(
        [
            scores_of(query3, whole_keys),
            jnp.where(allowed_self[None], scores_of(query3, keys), -jnp.inf),
        ],
        axis=2,
    )
    top = jnp.max(scores, axis=2, keepdims=True)
    lse = top + jnp.log(jnp.sum(jnp.exp(scores - top), axis=2, keepdims=True))
    prob = jnp.where(rowlive, jnp.exp(scores - lse), 0.0)
    prob_b = prob.astype(jnp.bfloat16)
    all_values = jnp.concatenate([whole_values, values], axis=0)
    attn_out = jnp.einsum(
        "hqk,khd->qhd", prob_b, split_heads(all_values), preferred_element_type=jnp.float32
    ).astype(jnp.bfloat16)
    delta = jnp.transpose(jnp.sum(cot3.astype(jnp.float32) * attn_out.astype(jnp.float32), axis=2))[
        :, :, None
    ]
    all_keys = jnp.concatenate([whole_keys, keys], axis=0)
    dprob = jnp.einsum(
        "qhd,khd->hqk", cot3, split_heads(all_values), preferred_element_type=jnp.float32
    )
    dscore = (prob * (dprob - delta)).astype(jnp.bfloat16)
    query_raw = jnp.einsum(
        "hqk,khd->qhd", dscore, split_heads(all_keys), preferred_element_type=jnp.float32
    )
    key_all = (
        jnp.einsum("hqk,qhd->khd", dscore, query3, preferred_element_type=jnp.float32) * scale
    ).reshape(-1, width)
    value_all = jnp.einsum(
        "hqk,qhd->khd", prob_b, cot3, preferred_element_type=jnp.float32
    ).reshape(-1, width)
    prompt_key_part = key_all[:prompt_rows]
    prompt_value_part = value_all[:prompt_rows]
    key_self = key_all[prompt_rows:]
    value_self = value_all[prompt_rows:]
    query_grad = (query_raw * scale).reshape(slots, width).astype(jnp.bfloat16)
    prompt_key_grad, prompt_value_grad = (
        lax.psum_scatter(
            prompt_key_part.astype(jnp.bfloat16), "resp", scatter_dimension=0, tiled=True
        ).astype(jnp.float32),
        lax.psum_scatter(
            prompt_value_part.astype(jnp.bfloat16), "resp", scatter_dimension=0, tiled=True
        ).astype(jnp.float32),
    )
    return (
        query_grad,
        key_self.astype(jnp.bfloat16),
        value_self.astype(jnp.bfloat16),
        prompt_key_grad.astype(jnp.bfloat16),
        prompt_value_grad.astype(jnp.bfloat16),
    )


def solution(mesh):
    in_specs = (
        P(("dp", "resp"), None),
        P(("dp", "resp"), None),
        P(("dp", "resp"), None),
        P(("dp", "resp"), None),
        P(("dp", "resp"), None),
        P(("dp", "resp"), None),
        P(("dp", "resp"), None),
    )
    out_specs = (
        P(("dp", "resp"), None),
        P(("dp", "resp"), None),
        P(("dp", "resp"), None),
        P(("dp", "resp"), None),
        P(("dp", "resp"), None),
    )
    return jax.shard_map(
        per_device, mesh=mesh, in_specs=in_specs, out_specs=out_specs, check_vma=False
    )
```

profile of v0, /device:TPU:1, one launch (start us, length us, event | category | flops | bytes accessed | tf_op | source)
XLA Modules:
  0.0 169.4 jit_solution(17739599142041365923)
XLA Ops:
  7.2 0.9 reduce-window.4
  9.4 23.2 %all_gather.6 = bf16[128,2560]{1,0:T(8,128)(2,1)S(1)} all-gather(bf16[8,2560]{1,0:T(8,128)(2,1)} %param.12), channel_id=1, replica_groups=mesh['dp'=32,'resp'=16] {'resp'}, dimensions={0}, use_global_device_ids=true | all-gather | bytes 696320 | tf_op jit(solution)/shard_map/all_gather | solution.py:41
  32.6 1.1 copy.79
  34.1 1.1 copy.87
  35.1 1.1 copy.82
  36.3 1.6 fusion.18
  40.5 1.4 fusion.16
  41.9 2.2 %copy.97 = bf16[128,2560]{1,0:T(8,128)(2,1)} copy(bf16[128,2560]{0,1:T(8,128)(2,1)} %bitcast.50) | data formatting | bytes 1310720 | tf_op jit(solution)/shard_map/convert_element_type | solution.py:87
  44.1 2.2 %copy.86 = bf16[128,2560]{0,1:T(8,128)(2,1)} copy(bf16[128,2560]{1,0:T(8,128)(2,1)} %param.9) | data formatting | bytes 1310720 | tf_op args[2]
  46.3 19.0 %all_gather.7 = bf16[128,2560]{1,0:T(8,128)(2,1)} all-gather(bf16[8,2560]{1,0:T(8,128)(2,1)S(1)} %copy-done.11), channel_id=1, replica_groups=mesh['dp'=32,'resp'=16] {'resp'}, dimensions={0}, use_global_device_ids=true | all-gather | bytes 696320 | tf_op jit(solution)/shard_map/all_gather | solution.py:42
  65.3 2.2 %copy.85 = bf16[128,2560]{0,1:T(8,128)(2,1)} copy(bf16[128,2560]{1,0:T(8,128)(2,1)} %all_gather.7) | data formatting | bytes 1310720 | tf_op jit(solution)/shard_map/all_gather | solution.py:42
  67.5 1.6 pad_maximum_fusion.2
  70.0 2.3 %fusion = bf16[20,128,256]{1,2,0:T(8,128)(2,1)S(1)} fusion(bf16[256,20,128]{0,2,1:T(8,128)(2,1)S(1)} %bitcast.55, bf16[128,20,128]{0,2,1:T(8,128)(2,1)S(1)} %bitcast.58, f32[20,128,128]{1,2,0:T(8,128)S(1)} %copy-done.2, f32[20,128,128]{1,2,0:T(8,128)} %copy-done, f32[20,128]{1,0:T(8,128)S(1)} %bitcast.60, f32[20,128]{1,0:T(8,128)S(1)} %log_add_fusion, ...), kind=kOutput, calls=%fused_computation.2 | convolution fusion | flops 171704320 | bytes 5918848 | tf_op jit(solution)/shard_map/qhd,khd->hqk/dot_general | solution.py:64
  72.8 1.2 fusion.17
  74.0 1.1 copy.96
  75.2 1.1 pad_maximum_fusion.1
  76.3 1.6 copy.77
  77.9 1.4 fusion.10
  79.3 1.5 copy.93
  80.8 1.1 copy.98
  81.9 1.1 copy.99
  83.0 1.1 copy.100
  84.1 16.6 %reduce-scatter.5.cloned.1.call-done = bf16[8,2560]{1,0:T(8,128)(2,1)} async-done(((bf16[128,2560]{1,0:T(8,128)(2,1)}), bf16[8,2560]{1,0:T(8,128)(2,1)}) %reduce-scatter.5.cloned.1.call-update) | async-done | bytes 40976 | tf_op jit(solution)/shard_map/reduce_scatter | solution.py:86
  100.7 61.8 %reduce-scatter.3.cloned.1.call-done = bf16[8,2560]{1,0:T(8,128)(2,1)} async-done(((bf16[128,2560]{1,0:T(8,128)(2,1)}), bf16[8,2560]{1,0:T(8,128)(2,1)}) %reduce-scatter.3.cloned.1.call-update) | async-done | bytes 40976 | tf_op jit(solution)/shard_map/reduce_scatter | solution.py:83
  (40 shorter events, 5.9 us)
Async XLA Ops:
  7.2 26.6 %copy-start.7 = (bf16[128,2560]{1,0:T(8,128)(2,1)S(1)}, bf16[128,2560]{1,0:T(8,128)(2,1)}, u32[]{:S(2)}) copy-start(bf16[128,2560]{1,0:T(8,128)(2,1)} %param.7) | copy-start | bytes 1966084
  7.2 93.5 %reduce-scatter.5.cloned.1.call-start = ((), (), s32[]{:S(2)}) async-start(), calls=%async_computation.3 | async-start | bytes 696320 | tf_op jit(solution)/shard_map/reduce_scatter | solution.py:86
  32.6 1.4 copy-start.8
  33.7 1.4 copy-start.3
  36.3 1.6 copy-start.6
  37.9 31.1 %copy-start = (f32[20,128,128]{1,2,0:T(8,128)}, f32[20,128,128]{1,2,0:T(8,128)S(1)}, u32[]{:S(2)}) copy-start(f32[20,128,128]{1,2,0:T(8,128)S(1)} %get-tuple-element.30) | copy-start | bytes 3932164
  38.3 1.1 copy-start.1
  38.4 1.6 copy-start.9
  44.1 2.2 %copy-start.11 = (bf16[8,2560]{1,0:T(8,128)(2,1)S(1)}, bf16[8,2560]{1,0:T(8,128)(2,1)}, u32[]{:S(2)}) copy-start(bf16[8,2560]{1,0:T(8,128)(2,1)} %param.13) | copy-start | bytes 122884
  44.1 118.5 %reduce-scatter.3.cloned.1.call-start = ((), (), s32[]{:S(2)}) async-start(), calls=%async_computation.2 | async-start | bytes 696320 | tf_op jit(solution)/shard_map/reduce_scatter | solution.py:83
  67.4 1.7 %copy-start.2 = (f32[20,128,128]{1,2,0:T(8,128)S(1)}, f32[20,128,128]{1,2,0:T(8,128)}, u32[]{:S(2)}) copy-start(f32[20,128,128]{1,2,0:T(8,128)} %copy-done.1) | copy-start | bytes 3932164
  67.4 1.9 %copy-start.10 = (bf16[128,2560]{0,1:T(8,128)(2,1)S(1)}, bf16[128,2560]{0,1:T(8,128)(2,1)}, u32[]{:S(2)}) copy-start(bf16[128,2560]{0,1:T(8,128)(2,1)} %copy.87) | copy-start | bytes 1966084
  79.3 2.6 %copy-start.5 = (bf16[128,20,128]{0,2,1:T(8,128)(2,1)S(1)}, bf16[128,20,128]{0,2,1:T(8,128)(2,1)}, u32[]{:S(2)}) copy-start(bf16[128,20,128]{0,2,1:T(8,128)(2,1)} %get-tuple-element.28) | copy-start | bytes 1966084
  80.8 2.2 %copy-start.4 = (bf16[128,20,128]{0,2,1:T(8,128)(2,1)S(1)}, bf16[128,20,128]{0,2,1:T(8,128)(2,1)}, u32[]{:S(2)}) copy-start(bf16[128,20,128]{0,2,1:T(8,128)(2,1)} %get-tuple-element.26) | copy-start | bytes 1966084
Sparse Core Ops, SparseCore 0:
  44.2 56.4 reduce-scatter.4
  104.3 58.1 reduce-scatter.2
where the time goes:
time: 171 us; the launch traced here: 169 us
  waiting for transfers between devices  78.5 us (46%)
  blocking collectives  42.2 us (25%)
  local copies, waits for them, and re-layouts  22.2 us (13%)
  between operations  14.2 us (8%)
  matrix products  7.38 us (4%)
  other arithmetic  4.82 us (3%)
    reduce_scatter x1, waiting for transfers between devices, per_device(): lax.psum_scatter(prompt_key_part.astype(jnp.bfloat16), 'resp', scatter_di...  61.8 us
    all_gather x1, blocking collectives, per_device(): lax.all_gather(prompt_keys, 'resp', axis=0, tiled=True)  23.2 us
    all_gather x1, blocking collectives, per_device(): lax.all_gather(prompt_values, 'resp', axis=0, tiled=True)  19 us
    reduce_scatter x1, waiting for transfers between devices, per_device(): lax.psum_scatter(prompt_value_part.astype(jnp.bfloat16), 'resp', scatter_...  16.6 us
    unnamed x31, local copies, waits for them, and re-layouts  9.39 us
  transfers between devices with their start and end apart: 2, of which 2 were waited for; matrix products, arithmetic and copies ran while one was open for 12% of the time, Pallas kernels for 0%

commit v1 on v0

v1 whole, which is shorter than its diff:
```python
import functools

import jax
import jax.numpy as jnp
from jax import lax
from jax.experimental import pallas as pl
from jax.experimental.pallas import tpu as pltpu
from jax.sharding import PartitionSpec as P

HD = 128
CHIPS = 8
HPC = 5
SCALE = HD ** (-0.5)
LOG2E = 1.4426950408889634
MASKED = -1e30
MESH = pl.DeviceIdType.MESH
NT = (((1,), (1,)), ((), ()))
NN = (((1,), (0,)), ((), ()))
TN = (((0,), (0,)), ((), ()))
F32 = jnp.float32
BF16 = jnp.bfloat16


def mm(a, b, dims):
    return lax.dot_general(a, b, dims, preferred_element_type=F32)


SLOT = {0: 0, 2: 1, -2: 2, 1: 3, -1: 4, 3: 5, -3: 6, 4: 7, -4: 7}


def half(ch, way):
    cut = HPC // 2 + (HPC % 2) * (ch % 2)
    return pl.ds(0, cut * HD) if way == 1 else pl.ds(cut * HD, (HPC - cut) * HD)


def kernel(
    nc,
    len_hbm, q_hbm, k_hbm, v_hbm, co_hbm, pk_hbm, pv_hbm,
    dq_ref, dk_ref, dv_ref, pg_ref,
    len_ref, pk_ref, pv_ref, q_ref, co_ref, ka_ref, va_ref,
    gat_ref, part_ref, sib_ref, tx_ref, mid_ref, end_ref,
    bias_ref, e_ref, dp_ref, ds_ref, stat_ref,
    in_sem,
    ag_send, ag_recv, ag2_send, ag2_recv,
    rs_send, rs_recv, rs2_send, rs2_recv,
):
    width = HPC * HD
    me = lax.axis_index("resp")
    y = me // 2
    core = lax.rem(me, 2)
    sibling = 2 * y + (1 - core)

    def away(offset):
        return 2 * lax.rem(y + CHIPS + offset, CHIPS) + core

    def remote(src, dst, send, recv, to):
        return pltpu.make_async_remote_copy(
            src_ref=src, dst_ref=dst, send_sem=send, recv_sem=recv,
            device_id={"resp": to}, device_id_type=MESH,
        )

    lower = pl.ds(128, 128)
    loads = [
        pltpu.make_async_copy(pk_hbm, pk_ref, in_sem.at[0]),
        pltpu.make_async_copy(pv_hbm, pv_ref, in_sem.at[1]),
        pltpu.make_async_copy(q_hbm, q_ref, in_sem.at[2]),
        pltpu.make_async_copy(k_hbm, ka_ref.at[lower], in_sem.at[3]),
        pltpu.make_async_copy(co_hbm, co_ref, in_sem.at[4]),
        pltpu.make_async_copy(v_hbm, va_ref.at[lower], in_sem.at[5]),
        pltpu.make_async_copy(len_hbm, len_ref, in_sem.at[6]),
    ]
    for load in loads:
        load.start()

    barrier = pltpu.get_barrier_semaphore()
    for other in (sibling, away(1), away(-1), away(2), away(-2)):
        pl.semaphore_signal(barrier, inc=1, device_id={"resp": other}, device_id_type=MESH)

    loads[0].wait()
    loads[1].wait()
    own = jnp.concatenate([pk_ref[...].astype(F32), pv_ref[...].astype(F32)], axis=0).astype(BF16)
    for ch in range(nc):
        gat_ref[ch, 0, 0] = own[:, ch * width:(ch + 1) * width]

    pl.semaphore_wait(barrier, 5)

    def ag_copy(ch, way, kind):
        n = 2 if kind != 2 else 0 if way == 1 else 1
        if kind <= 2:
            src, dst = gat_ref.at[ch, 0, 0], gat_ref.at[ch, 0, SLOT[-way * kind]]
        else:
            src, dst = gat_ref.at[ch, 0, SLOT[-way * 2]], gat_ref.at[ch, 0, SLOT[-way * kind]]
            if kind == 4:
                src, dst = src.at[:, half(ch, way)], dst.at[:, half(ch, way)]
        return remote(src, dst, ag_send.at[ch], ag_recv.at[ch, n],
                      away(way * (2 if kind in (2, 4) else 1)))

    def ag_far(ch):
        for way in (1, -1):
            ag_copy(ch, way, 2).start()

    def ag_near(ch):
        for way in (1, -1):
            ag_copy(ch, way, 1).start()

    def ag_second(ch):
        for way in (1, -1):
            ag_copy(ch, way, 2).wait_recv()
            ag_copy(ch, way, 4).start()
            ag_copy(ch, way, 3).start()

    def ag_pair(ch):
        return remote(gat_ref.at[ch, 0], gat_ref.at[ch, 1], ag2_send.at[ch], ag2_recv.at[ch], sibling)

    def ag_third(ch):
        rest = gat_ref.at[ch, 0, pl.ds(3, 5)]
        remote(rest, rest, ag_send.at[ch], ag_recv.at[ch, 2], sibling).wait_recv()
        ag_pair(ch).start()

    def ag_sent(ch):
        every = gat_ref.at[ch, 0, pl.ds(1, 7)]
        remote(every, every, ag_send.at[ch], ag_recv.at[ch, 2], sibling).wait_send()
        ag_pair(ch).wait_send()

    ag_far(0)
    ag_near(0)
    for ch in range(1, min(nc, 3)):
        ag_far(ch)

    loads[6].wait()
    ends = [len_ref[0, 0]]
    for r in range(1, 4):
        ends.append(ends[-1] + len_ref[0, r])
    key_at = lax.broadcasted_iota(jnp.int32, (128, 128), 0)
    query_at = lax.broadcasted_iota(jnp.int32, (128, 128), 1)

    def segment_of(place):
        return sum((place >= end).astype(jnp.int32) for end in ends)

    allowed = (segment_of(key_at) == segment_of(query_at)) & (key_at <= query_at)
    allowed = allowed & (query_at < ends[3])
    bias_ref[...] = jnp.where(allowed, 0.0, MASKED).astype(F32)
    live = lax.broadcasted_iota(jnp.int32, (1, 128), 1) < ends[3]

    def in_turn(ch, first, rest):
        ahead = first(ch * HPC)
        for h in range(ch * HPC, (ch + 1) * HPC):
            now = ahead
            if h + 1 < (ch + 1) * HPC:
                ahead = first(h + 1)
            rest(h, *now)

    def columns(h):
        return pl.ds(h * HD, HD)

    def own_keys(ch):
        def first(h):
            cols = columns(h)
            return mm(ka_ref[lower, cols], q_ref[:, cols], NT), mm(va_ref[lower, cols], co_ref[:, cols], NT)

        def rest(h, s, dp):
            s = s * (SCALE * LOG2E) + bias_ref[...]
            m = jnp.max(s, axis=0, keepdims=True)
            e = jnp.exp2(s - m)
            e_ref[h] = e
            dp_ref[h] = dp
            stat_ref[h, 0:1] = m
            stat_ref[h, 1:2] = jnp.sum(e, axis=0, keepdims=True)
            stat_ref[h, 2:3] = jnp.sum(e * dp, axis=0, keepdims=True)

        in_turn(ch, first, rest)

    def prompt_keys(ch):
        def inner(h):
            return pl.ds((h - ch * HPC) * HD, HD)

        def first(h):
            cols = columns(h)
            both = gat_ref[ch, :, :, :, inner(h)].reshape(16, 16, HD).astype(F32)
            kp = both[:, :8].reshape(128, HD).astype(BF16)
            vp = both[:, 8:].reshape(128, HD).astype(BF16)
            ka_ref[0:128, cols] = kp
            return mm(kp, q_ref[:, cols], NT), mm(vp, co_ref[:, cols], NT)

        def rest(h, s, dp):
            cols = columns(h)
            s = s * (SCALE * LOG2E)
            m_own = stat_ref[h, 0:1]
            m = jnp.maximum(jnp.max(s, axis=0, keepdims=True), m_own)
            e = jnp.exp2(s - m)
            a = jnp.exp2(m_own - m)
            total = jnp.sum(e, axis=0, keepdims=True) + a * stat_ref[h, 1:2]
            inv = jnp.where(live, 1.0 / total, 0.0)
            delta = (jnp.sum(e * dp, axis=0, keepdims=True) + a * stat_ref[h, 2:3]) * inv
            p = e * inv
            ds = (p * (dp - delta)).astype(BF16)
            ds_ref[h] = ds
            stat_ref[h, 3:4] = a * inv
            stat_ref[h, 4:5] = delta
            gk = (mm(ds, q_ref[:, cols], NN) * SCALE).reshape(16, 8, HD)
            gv = mm(p.astype(BF16), co_ref[:, cols], NN).reshape(16, 8, HD)
            part_ref[ch, :, :, :, inner(h)] = (
                jnp.concatenate([gk, gv], axis=1).astype(BF16).reshape(2, CHIPS, 16, HD))

        in_turn(ch, first, rest)

    def gradients(ch):
        def first(h):
            p = e_ref[h] * stat_ref[h, 3:4]
            ds = (p * (dp_ref[h] - stat_ref[h, 4:5])).astype(BF16)
            return p.astype(BF16), ds

        def rest(h, p, ds):
            cols = columns(h)
            dv_ref[:, cols] = mm(p, co_ref[:, cols], NN).astype(BF16)
            dk_ref[:, cols] = (mm(ds, q_ref[:, cols], NN) * SCALE).astype(BF16)
            both = jnp.concatenate([ds_ref[h], ds], axis=0)
            dq_ref[:, cols] = (mm(both, ka_ref[:, cols], TN) * SCALE).astype(BF16)

        in_turn(ch, first, rest)

    def rs_pair(ch):
        return remote(part_ref.at[ch, 1], sib_ref.at[ch], rs2_send.at[ch], rs2_recv.at[ch], sibling)

    def rs_copy(ch, way, kind):
        w = 0 if way == 1 else 1
        src = tx_ref.at[ch, 4 * w + kind - 1]
        if kind <= 2:
            dst, sem = end_ref.at[ch, 2 * w + kind - 1], rs_recv.at[ch, 0]
        else:
            dst, sem = mid_ref.at[ch, w, kind - 3], rs_recv.at[ch, 2 * w + kind - 2]
        if kind == 4:
            src, dst = src.at[:, half(ch, way)], dst.at[:, half(ch, way)]
        return remote(src, dst, rs_send.at[ch], sem, away(way * (2 if kind in (2, 4) else 1)))

    def rs_sent(ch):
        every = tx_ref.at[ch, pl.ds(0, 7)]
        remote(every, every, rs_send.at[ch], rs_recv.at[ch, 0], sibling).wait_send()
        rs_pair(ch).wait_send()

    def chip_sum(ch, offset):
        slot = SLOT[offset]
        return part_ref[ch, 0, slot].astype(F32) + sib_ref[ch, slot].astype(F32)

    def rs_first(ch):
        rs_pair(ch).wait_recv()
        far = chip_sum(ch, 4)
        for w, way in enumerate((1, -1)):
            cols = half(ch, way)
            tx_ref[ch, 4 * w + 3, :, cols] = far[:, cols.start:cols.start + cols.size].astype(BF16)
            rs_copy(ch, way, 4).start()
            for kind in (3, 1):
                tx_ref[ch, 4 * w + kind - 1] = chip_sum(ch, way * kind).astype(BF16)
                rs_copy(ch, way, kind).start()

    def rs_second(ch):
        for w, way in enumerate((1, -1)):
            cols = half(ch, way)
            rs_copy(ch, way, 3).wait_recv()
            rs_copy(ch, way, 4).wait_recv()
            total = chip_sum(ch, way * 2) + mid_ref[ch, w, 0].astype(F32)
            tx_ref[ch, 4 * w + 1] = total.astype(BF16)
            part = total[:, cols.start:cols.start + cols.size]
            tx_ref[ch, 4 * w + 1, :, cols] = (
                part + mid_ref[ch, w, 1, :, cols].astype(F32)).astype(BF16)
            rs_copy(ch, way, 2).start()

    def rs_third(ch):
        last = end_ref.at[ch]
        remote(last, last, rs_send.at[ch], rs_recv.at[ch, 0], sibling).wait_recv()
        total = chip_sum(ch, 0)
        for n in range(4):
            total = total + end_ref[ch, n].astype(F32)
        pg_ref[:, ch * width:(ch + 1) * width] = total.astype(BF16)

    for n in (2, 3, 4, 5):
        loads[n].wait()
    def prompt_step(ch):
        ag_pair(ch).wait_recv()
        prompt_keys(ch)
        rs_pair(ch).start()

    for step, ch in (
        (own_keys, 0), (ag_second, 0), (ag_near, 1), (ag_far, 3),
        (own_keys, 1), (ag_second, 1), (ag_near, 2),
        (own_keys, 2), (ag_second, 2), (ag_near, 3), (ag_third, 0),
        (own_keys, 3), (ag_second, 3), (ag_third, 1), (prompt_step, 0),
        (ag_third, 2), (prompt_step, 1),
        (rs_first, 0), (ag_third, 3), (prompt_step, 2),
        (rs_first, 1), (prompt_step, 3),
        (rs_first, 2), (rs_second, 0), (gradients, 0),
        (rs_first, 3), (rs_second, 1), (gradients, 1),
        (rs_second, 2), (gradients, 2),
        (rs_second, 3), (gradients, 3),
        (ag_sent, 0), (ag_sent, 1), (ag_sent, 2), (ag_sent, 3),
        (rs_third, 0), (rs_third, 1), (rs_third, 2),
        (rs_sent, 0), (rs_sent, 1), (rs_sent, 2), (rs_third, 3), (rs_sent, 3),
    ):
        if ch < nc:
            step(ch)


def finish(dq_in, dk_in, dv_in, pg_in, dq, dk, dv, gk, gv, gk_ref, gv_ref, sem):
    copies = []
    for n, (src, dst) in enumerate(((dq_in, dq), (dk_in, dk), (dv_in, dv))):
        for part in range(4):
            rows = pl.ds(part * 32, 32)
            copies.append(pltpu.make_async_copy(src.at[rows], dst.at[rows], sem.at[n, part]))
    for copy in copies:
        copy.start()
    both = pg_in[...].astype(F32)
    gk_ref[...] = both[:8].astype(BF16)
    gv_ref[...] = both[8:].astype(BF16)
    for n, (src, dst) in enumerate(((gk_ref, gk), (gv_ref, gv))):
        copies.append(pltpu.make_async_copy(src, dst, sem.at[3, n]))
        copies[-1].start()
    for copy in copies:
        copy.wait()


def per_device(queries, keys, values, cotangent, lengths, prompt_keys, prompt_values):
    slots, width = queries.shape
    n_heads = width // HD
    nc = n_heads // HPC
    cw = HPC * HD
    anywhere = pl.BlockSpec(memory_space=pl.ANY)
    vmem = pl.BlockSpec(memory_space=pltpu.VMEM)
    dma = pltpu.SemaphoreType.DMA
    big = jax.ShapeDtypeStruct((slots, width), BF16)
    small = jax.ShapeDtypeStruct((8, width), BF16)
    dq, dk, dv, pg = pl.pallas_call(
        functools.partial(kernel, nc),
        out_shape=(pltpu.VMEM((slots, width), BF16),) * 3 + (pltpu.VMEM((16, width), BF16),),
        in_specs=[pl.BlockSpec(memory_space=pltpu.HBM)] * 7,
        out_specs=(vmem,) * 4,
        scratch_shapes=[
            pltpu.SMEM((1, 4), jnp.int32),
            pltpu.VMEM((8, width), BF16),
            pltpu.VMEM((8, width), BF16),
            pltpu.VMEM((slots, width), BF16),
            pltpu.VMEM((slots, width), BF16),
            pltpu.VMEM((256, width), BF16),
            pltpu.VMEM((256, width), BF16),
            pltpu.VMEM((nc, 2, CHIPS, 16, cw), BF16),
            pltpu.VMEM((nc, 2, CHIPS, 16, cw), BF16),
            pltpu.VMEM((nc, CHIPS, 16, cw), BF16),
            pltpu.VMEM((nc, 8, 16, cw), BF16),
            pltpu.VMEM((nc, 2, 2, 16, cw), BF16),
            pltpu.VMEM((nc, 4, 16, cw), BF16),
            pltpu.VMEM((128, 128), F32),
            pltpu.VMEM((n_heads, 128, 128), F32),
            pltpu.VMEM((n_heads, 128, 128), F32),
            pltpu.VMEM((n_heads, 128, 128), BF16),
            pltpu.VMEM((n_heads, 8, 128), F32),
            dma((7,)),
            dma((nc,)), dma((nc, 3)), dma((nc,)), dma((nc,)),
            dma((nc,)), dma((nc, 5)), dma((nc,)), dma((nc,)),
        ],
        compiler_params=pltpu.CompilerParams(
            collective_id=0, has_side_effects=True, vmem_limit_bytes=40 * 1024 * 1024
        ),
    )(*(
        pltpu.with_memory_space_constraint(x, pltpu.HBM)
        for x in (lengths, queries, keys, values, cotangent, prompt_keys, prompt_values)
    ))
    return pl.pallas_call(
        finish,
        out_shape=(big, big, big, small, small),
        in_specs=[anywhere, anywhere, anywhere, vmem],
        out_specs=(anywhere,) * 5,
        scratch_shapes=[pltpu.VMEM((8, width), BF16), pltpu.VMEM((8, width), BF16), dma((4, 4))],
        compiler_params=pltpu.CompilerParams(vmem_limit_bytes=8 * 1024 * 1024),
    )(*(pltpu.with_memory_space_constraint(x, pltpu.VMEM) for x in (dq, dk, dv, pg)))


def solution(mesh):
    spec = P(("dp", "resp"), None)
    return jax.shard_map(
        per_device, mesh=mesh, in_specs=(spec,) * 7, out_specs=(spec,) * 5, check_vma=False
    )
```

time: 171 us -> 34.6 us (0.20)
  waiting for transfers between devices: 78.5 us -> 0 us
  blocking collectives: 42.2 us -> 0 us
  Pallas kernels: 0 us -> 33.8 us
  local copies, waits for them, and re-layouts: 22.2 us -> 0 us
  between operations: 14.2 us -> 0.64 us
  matrix products: 7.38 us -> 0 us
  other arithmetic: 4.82 us -> 0 us
    reduce_scatter x2 -> x0, waiting for transfers between devices: 78.5 us -> none  [the longest x1 61.8 us: per_device(): lax.psum_scatter(prompt_key_part.astype(jnp.bfloat16), 'resp', scatter_di...]
    all_gather x2 -> x0, blocking collectives: 42.2 us -> none  [the longest x1 23.2 us: per_device(): lax.all_gather(prompt_keys, 'resp', axis=0, tiled=True)]
    pallas_call x0 -> x2, Pallas kernels: none -> 33.8 us  [the longest x1 32.4 us: per_device(): pl.pallas_call(functools.partial(kernel, nc), out_shape=(pltpu.VMEM((slot...]
    unnamed x31 -> x0, local copies, waits for them, and re-layouts: 9.39 us -> none
    dot_general x7 -> x0, matrix products: 7.38 us -> none  [the longest x1 2.28 us: per_device(): jnp.einsum('qhd,khd->hqk', cot3, split_heads(all_values), preferred_eleme...]
    convert_element_type x3 -> x0, local copies, waits for them, and re-layouts: 4.76 us -> none  [the longest x1 2.17 us: per_device(): prompt_value_part.astype(jnp.bfloat16)]
    all_gather x2 -> x0, local copies, waits for them, and re-layouts: 3.24 us -> none  [the longest x1 2.17 us: per_device(): lax.all_gather(prompt_values, 'resp', axis=0, tiled=True)]
    slice x3 -> x0, local copies, waits for them, and re-layouts: 3.21 us -> none  [the longest x1 1.43 us: per_device(): prompt_value_part = value_all[:prompt_rows]]
  transfers between devices with their start and end apart: 2 -> 0, of which waited for: 2 -> 0; matrix products, arithmetic and copies ran while one was open for 12% -> 0% of each run, Pallas kernels for 0% -> 0%
where the time goes in v1:
time: 34.6 us; the launch traced here: 34.5 us
  Pallas kernels  33.8 us (98%)
  between operations  0.64 us (2%)
    pallas_call x1, Pallas kernels, per_device(): pl.pallas_call(functools.partial(kernel, nc), out_shape=(pltpu.VMEM((slot...  32.4 us
    pallas_call x1, Pallas kernels, per_device(): pl.pallas_call(finish, out_shape=(big, big, big, small, small), in_specs=...  1.42 us

profile of v1, /device:TPU:1, one launch (start us, length us, event | category | flops | bytes accessed | tf_op | source)
XLA Modules:
  0.0 34.5 jit_solution(13329842899518052903)
XLA Ops:
  0.6 32.4 %shard_map.110 = (bf16[128,2560]{1,0:T(8,128)(2,1)S(1)}, bf16[128,2560]{1,0:T(8,128)(2,1)S(1)}, bf16[128,2560]{1,0:T(8,128)(2,1)S(1)}, bf16[16,2560]{1,0:T(8,128)(2,1)S(1)}) custom-call(s32[1,4]{1,0:T(1,128)} %len_hbm.1, bf16[128,2560]{1,0:T(8,128)(2,1)} %q_hbm.1, bf16[128,2560]{1,0:T(8,128)(2,1)} %k_hbm.1, bf16[128,2560]{1,0:T(8,128)(2,1)} %v_hbm.1, ...), custom_call_target="tpu_custom_call" | custom-call | tf_op jit(solution)/shard_map/pallas_call | solution.py:331
  33.1 1.4 %shard_map.111 = (bf16[128,2560]{1,0:T(8,128)(2,1)}, bf16[128,2560]{1,0:T(8,128)(2,1)}, bf16[128,2560]{1,0:T(8,128)(2,1)}, bf16[8,2560]{1,0:T(8,128)(2,1)}, bf16[8,2560]{1,0:T(8,128)(2,1)}) custom-call(bf16[128,2560]{1,0:T(8,128)(2,1)S(1)} %get-tuple-element.9.dq_in, bf16[128,2560]{1,0:T(8,128)(2,1)S(1)} %get-tuple-element.10.dk_in, ...), custom_call_target="tpu_custom_call" | custom-call | tf_op jit(solution)/shard_map/pallas_call | solution.py:366

commit v2 on v1

v2 whole, which is shorter than its diff:
```python
import functools

import jax
import jax.numpy as jnp
from jax import lax
from jax.experimental import pallas as pl
from jax.experimental.pallas import tpu as pltpu
from jax.sharding import PartitionSpec as P

HD = 128
CHIPS = 8
SCALE = HD ** (-0.5)
LOG2E = 1.4426950408889634
MASKED = -1e30
MESH = pl.DeviceIdType.MESH
NT = (((1,), (1,)), ((), ()))
NN = (((1,), (0,)), ((), ()))
TN = (((0,), (0,)), ((), ()))
F32 = jnp.float32
BF16 = jnp.bfloat16


def mm(a, b, dims):
    return lax.dot_general(a, b, dims, preferred_element_type=F32)


SLOT = {0: 0, 2: 1, -2: 2, 1: 3, -1: 4, 3: 5, -3: 6, 4: 7, -4: 7}


def chunks_of(heads):
    if heads == 10:
        return (0, 2, 5, 8, 10)
    return tuple(range(0, heads, 2)) + (heads,)


def kernel(
    cuts,
    len_hbm, q_hbm, k_hbm, v_hbm, co_hbm, pk_hbm, pv_hbm,
    out_ref, pg_ref,
    len_ref, pk_ref, pv_ref, q_ref, co_ref, ka_ref, va_ref,
    gat_ref, other_ref, part_ref, mid_ref, tx_ref, end_ref,
    bias_ref, e_ref, dp_ref, ds_ref, stat_ref, grad_ref,
    in_sem, swap_send, swap_recv, own_sem, grad_sem,
    ag_send, ag_recv, rs_send, rs_recv, rs_own,
):
    nc = len(cuts) - 1
    wide = cuts[-1] * HD
    me = lax.axis_index("resp")
    y = me // 2
    core = lax.rem(me, 2)
    sibling = 2 * y + (1 - core)
    mine = pl.ds(pl.multiple_of(core * wide, wide), wide)
    theirs = pl.ds(pl.multiple_of((1 - core) * wide, wide), wide)

    def away(offset, other=0):
        return 2 * lax.rem(y + CHIPS + offset, CHIPS) + (1 - core if other else core)

    def remote(src, dst, send, recv, to):
        return pltpu.make_async_remote_copy(
            src_ref=src, dst_ref=dst, send_sem=send, recv_sem=recv,
            device_id={"resp": to}, device_id_type=MESH,
        )

    def span(ch):
        return pl.ds(cuts[ch] * HD, (cuts[ch + 1] - cuts[ch]) * HD)

    def half(ch, way):
        lo, hi = cuts[ch], cuts[ch + 1]
        cut = lo + (hi - lo + ch % 2) // 2
        return pl.ds(lo * HD, (cut - lo) * HD) if way == 1 else pl.ds(cut * HD, (hi - cut) * HD)

    key_rows = (pl.ds(0, 128), pl.ds(256, 128))
    prompt_rows = pl.ds(128, 128)

    loads = [
        pltpu.make_async_copy(pk_hbm, pk_ref, in_sem.at[0]),
        pltpu.make_async_copy(pv_hbm, pv_ref, in_sem.at[1]),
        pltpu.make_async_copy(len_hbm, len_ref, in_sem.at[2]),
        pltpu.make_async_copy(k_hbm.at[:, mine], ka_ref.at[key_rows[0]], in_sem.at[3]),
        pltpu.make_async_copy(q_hbm.at[:, mine], q_ref.at[0], in_sem.at[4]),
        pltpu.make_async_copy(v_hbm.at[:, mine], va_ref.at[0], in_sem.at[5]),
        pltpu.make_async_copy(co_hbm.at[:, mine], co_ref.at[0], in_sem.at[6]),
    ]
    for load in loads:
        load.start()

    barrier = pltpu.get_barrier_semaphore()
    partners = [sibling] + [away(o, other) for o in (1, -1, 2, -2) for other in (0, 1)]
    for partner in partners:
        pl.semaphore_signal(barrier, inc=1, device_id={"resp": partner}, device_id_type=MESH)

    loads[0].wait()
    loads[1].wait()
    own = jnp.concatenate([pk_ref[...].astype(F32), pv_ref[...].astype(F32)], axis=0)
    first_core = core == 0
    gat_ref[0, 0] = jnp.where(first_core, own[:, :wide], own[:, wide:]).astype(BF16)
    other_ref[...] = jnp.where(first_core, own[:, wide:], own[:, :wide]).astype(BF16)

    pl.semaphore_wait(barrier, len(partners))

    def ag_send_own(ch, kind):
        cols = span(ch)
        for way in (1, -1):
            sem = 2 if kind == 1 else 0 if way == 1 else 1
            for other in (0, 1):
                src = other_ref.at[:, cols] if other else gat_ref.at[0, 0, :, cols]
                dst = gat_ref.at[SLOT[-way * kind], other, :, cols]
                remote(src, dst, ag_send.at[ch], ag_recv.at[ch, sem], away(way * kind, other)).start()

    def ag_far(ch):
        ag_send_own(ch, 2)

    def ag_near(ch):
        ag_send_own(ch, 1)

    def ag_second(ch):
        for way in (1, -1):
            slot = SLOT[-way * 2]
            block = gat_ref.at[slot, :, :, span(ch)]
            remote(block, block, ag_send.at[ch], ag_recv.at[ch, 0 if way == 1 else 1],
                   sibling).wait_recv()
            cols = half(ch, way)
            remote(gat_ref.at[slot, :, :, cols], gat_ref.at[SLOT[4], :, :, cols],
                   ag_send.at[ch], ag_recv.at[ch, 2], away(way * 2)).start()
            remote(block, gat_ref.at[SLOT[-way * 3], :, :, span(ch)],
                   ag_send.at[ch], ag_recv.at[ch, 2], away(way)).start()

    def ag_third(ch):
        rest = gat_ref.at[pl.ds(3, 5), :, :, span(ch)]
        remote(rest, rest, ag_send.at[ch], ag_recv.at[ch, 2], sibling).wait_recv()

    def ag_sent(ch):
        every = gat_ref.at[pl.ds(1, 7), :, :, span(ch)]
        remote(every, every, ag_send.at[ch], ag_recv.at[ch, 2], sibling).wait_send()

    own_block = remote(other_ref, gat_ref.at[0, 1], own_sem.at[0], own_sem.at[1], sibling)
    swaps = [
        remote(src, dst, swap_send.at[n], swap_recv.at[n], sibling)
        for n, (src, dst) in enumerate((
            (k_hbm.at[:, theirs], ka_ref.at[key_rows[1]]),
            (q_hbm.at[:, theirs], q_ref.at[1]),
            (v_hbm.at[:, theirs], va_ref.at[1]),
            (co_hbm.at[:, theirs], co_ref.at[1]),
            (bias_ref.at[0], bias_ref.at[1]),
        ))
    ]
    ag_far(0)
    ag_near(0)
    for ch in range(1, nc):
        ag_far(ch)
    own_block.start()
    for swap in swaps[:4]:
        swap.start()

    loads[2].wait()
    ends = [len_ref[0, 0]]
    for r in range(1, 4):
        ends.append(ends[-1] + len_ref[0, r])
    key_at = lax.broadcasted_iota(jnp.int32, (128, 128), 0)
    query_at = lax.broadcasted_iota(jnp.int32, (128, 128), 1)

    def segment_of(place):
        return sum((place >= end).astype(jnp.int32) for end in ends)

    allowed = (segment_of(key_at) == segment_of(query_at)) & (key_at <= query_at)
    allowed = allowed & (query_at < ends[3])
    bias_ref[0, 0:128] = jnp.where(allowed, 0.0, MASKED).astype(F32)
    bias_ref[0, 128:136] = jnp.where(query_at[0:8] < ends[3], 1.0, 0.0).astype(F32)
    swaps[4].start()
    for load in loads[3:]:
        load.wait()

    def in_turn(items, first, rest):
        ahead = first(*items[0])
        for n, item in enumerate(items):
            now = ahead
            if n + 1 < len(items):
                ahead = first(*items[n + 1])
            rest(*item, *now)

    def columns(h):
        return pl.ds(h * HD, HD)

    def heads(ch):
        return range(cuts[ch], cuts[ch + 1])

    def own_keys(ch, b):
        def first(h):
            cols = columns(h)
            return (mm(ka_ref[key_rows[b], cols], q_ref[b, :, cols], NT),
                    mm(va_ref[b, :, cols], co_ref[b, :, cols], NT))

        def rest(h, s, dp):
            s = s * (SCALE * LOG2E) + bias_ref[b, 0:128]
            m = jnp.max(s, axis=0, keepdims=True)
            e = jnp.exp2(s - m)
            e_ref[h, b] = e
            dp_ref[h, b] = dp
            lanes = pl.ds(b * 128, 128)
            stat_ref[h, 0:1, lanes] = m
            stat_ref[h, 1:2, lanes] = jnp.sum(e, axis=0, keepdims=True)
            stat_ref[h, 2:3, lanes] = jnp.sum(e * dp, axis=0, keepdims=True)

        in_turn([(h,) for h in heads(ch)], first, rest)

    def own_keys_0(ch):
        own_keys(ch, 0)

    def own_keys_1(ch):
        if ch == 0:
            for swap in swaps:
                swap.wait_recv()
        own_keys(ch, 1)

    def prompt_keys(ch):
        if ch == 0:
            own_block.wait_recv()
        ag_third(ch)
        live = jnp.concatenate([bias_ref[0, 128:129], bias_ref[1, 128:129]], axis=1)

        def first(h):
            cols = columns(h)
            both = gat_ref[:, :, :, cols].reshape(16, 16, HD).astype(F32)
            kp = both[:, :8].reshape(128, HD).astype(BF16)
            vp = both[:, 8:].reshape(128, HD).astype(BF16)
            ka_ref[prompt_rows, cols] = kp
            return (mm(kp, q_ref[:, :, cols].reshape(256, HD), NT),
                    mm(vp, co_ref[:, :, cols].reshape(256, HD), NT))

        def rest(h, s, dp):
            cols = columns(h)
            s = s * (SCALE * LOG2E)
            m_own = stat_ref[h, 0:1]
            m = jnp.maximum(jnp.max(s, axis=0, keepdims=True), m_own)
            e = jnp.exp2(s - m)
            a = jnp.exp2(m_own - m)
            total = jnp.sum(e, axis=0, keepdims=True) + a * stat_ref[h, 1:2]
            inv = live / total
            delta = (jnp.sum(e * dp, axis=0, keepdims=True) + a * stat_ref[h, 2:3]) * inv
            p = e * inv
            ds = (p * (dp - delta)).astype(BF16)
            ds_ref[h] = ds
            stat_ref[h, 3:4] = a * inv
            stat_ref[h, 4:5] = delta
            gk = mm(ds, q_ref[:, :, cols].reshape(256, HD), NN).reshape(16, 8, HD)
            gv = mm(p.astype(BF16), co_ref[:, :, cols].reshape(256, HD), NN).reshape(16, 8, HD)
            part_ref[:, :, :, cols] = (
                jnp.concatenate([gk, gv], axis=1).astype(BF16).reshape(CHIPS, 2, 16, HD))

        in_turn([(h,) for h in heads(ch)], first, rest)

    def give_back(ch):
        lo, size = cuts[ch] * HD, (cuts[ch + 1] - cuts[ch]) * HD
        at = pl.ds(pl.multiple_of(core * wide + lo, HD), size)
        return remote(grad_ref.at[:, :, span(ch)], out_ref.at[:, :, at],
                      grad_sem.at[0, ch], grad_sem.at[1, ch], sibling)

    def gradients(ch):
        def first(h, b):
            lanes = pl.ds(b * 128, 128)
            p = e_ref[h, b] * stat_ref[h, 3:4, lanes]
            ds = (p * (dp_ref[h, b] - stat_ref[h, 4:5, lanes])).astype(BF16)
            return p.astype(BF16), ds

        def rest(h, b, p, ds):
            cols = columns(h)
            dv = mm(p, co_ref[b, :, cols], NN).astype(BF16)
            dk = (mm(ds, q_ref[b, :, cols], NN) * SCALE).astype(BF16)
            dsp = ds_ref[h, :, pl.ds(b * 128, 128)]
            both = jnp.concatenate([ds, dsp] if b == 0 else [dsp, ds], axis=0)
            dq = (mm(both, ka_ref[pl.ds(b * 128, 256), cols], TN) * SCALE).astype(BF16)
            for n, grad in enumerate((dq, dk, dv)):
                if b == 0:
                    at = pl.ds(pl.multiple_of(core * wide + h * HD, HD), HD)
                    out_ref[n, :, at] = grad
                else:
                    grad_ref[n, :, cols] = grad

        in_turn([(h, b) for b in (1, 0) for h in heads(ch)], first, rest)
        give_back(ch).start()

    def end_at(kind, way, other):
        return 4 * other + 2 * (kind - 1) + (0 if way == 1 else 1)

    def rs_last(ch, kind, way, src):
        cols = span(ch)
        for other in (0, 1):
            remote(src.at[other, :, cols], end_ref.at[end_at(kind, way, other), :, cols],
                   rs_send.at[ch], rs_recv.at[ch, 0], away(way * kind, other)).start()

    def rs_mid(ch, kind, way):
        w = 0 if way == 1 else 1
        cols = half(ch, way) if kind == 4 else span(ch)
        return remote(part_ref.at[SLOT[way * kind], :, :, cols], mid_ref.at[w, kind - 3, :, :, cols],
                      rs_send.at[ch], rs_recv.at[ch, 2 * w + kind - 2],
                      away(way * (2 if kind == 4 else 1)))

    def rs_near(ch):
        cols = span(ch)
        return remote(part_ref.at[0, 1, :, cols], end_ref.at[8, :, cols],
                      rs_own.at[ch], rs_recv.at[ch, 0], sibling)

    def rs_first(ch):
        for way in (1, -1):
            rs_mid(ch, 4, way).start()
            rs_mid(ch, 3, way).start()
        for way in (1, -1):
            rs_last(ch, 1, way, part_ref.at[SLOT[way]])
        rs_near(ch).start()

    def rs_second(ch):
        cols = span(ch)
        for w, way in enumerate((1, -1)):
            some = half(ch, way)
            rs_mid(ch, 3, way).wait_recv()
            rs_mid(ch, 4, way).wait_recv()
            for other in (0, 1):
                total = part_ref[SLOT[way * 2], other, :, cols].astype(F32)
                total = total + mid_ref[w, 0, other, :, cols].astype(F32)
                tx_ref[w, other, :, cols] = total.astype(BF16)
                at = some.start - cols.start
                total = total[:, at:at + some.size] + mid_ref[w, 1, other, :, some].astype(F32)
                tx_ref[w, other, :, some] = total.astype(BF16)
            rs_last(ch, 2, way, tx_ref.at[w])

    def rs_third(ch):
        cols = span(ch)
        last = end_ref.at[:, :, cols]
        remote(last, last, rs_send.at[ch], rs_recv.at[ch, 0], sibling).wait_recv()
        same = part_ref[0, 0, :, cols].astype(F32)
        for n in range(4):
            same = same + end_ref[n, :, cols].astype(F32)
        other = end_ref[4, :, cols].astype(F32)
        for n in range(5, 9):
            other = other + end_ref[n, :, cols].astype(F32)
        for at, total in ((core, same), (1 - core, other)):
            total = jnp.concatenate([total[:8] * SCALE, total[8:]], axis=0)
            pg_ref[at, :, cols] = total.astype(BF16)

    def rs_sent(ch):
        every = part_ref.at[pl.ds(0, 7), :, :, span(ch)]
        remote(every, every, rs_send.at[ch], rs_recv.at[ch, 0], sibling).wait_send()
        rs_near(ch).wait_send()

    def swapped(ch):
        if ch == 0:
            own_block.wait_send()
            for swap in swaps:
                swap.wait_send()
        ag_sent(ch)

    def given(ch):
        give_back(ch).wait()

    for step, ch in (
        (own_keys_0, 0), (ag_second, 0), (ag_near, 1),
        (own_keys_0, 1), (ag_second, 1), (ag_near, 2),
        (own_keys_0, 2), (ag_second, 2), (ag_near, 3),
        (own_keys_0, 3), (ag_second, 3),
        (own_keys_1, 0), (own_keys_1, 1), (prompt_keys, 0), (rs_first, 0),
        (own_keys_1, 2), (prompt_keys, 1), (rs_first, 1),
        (own_keys_1, 3), (prompt_keys, 2), (rs_first, 2), (rs_second, 0),
        (prompt_keys, 3), (rs_first, 3), (rs_second, 1),
        (gradients, 0), (rs_second, 2), (gradients, 1), (rs_second, 3),
        (gradients, 2), (gradients, 3),
        (swapped, 0), (swapped, 1), (swapped, 2), (swapped, 3),
        (rs_third, 0), (rs_third, 1), (rs_third, 2),
        (rs_sent, 0), (rs_sent, 1), (rs_sent, 2), (given, 0), (given, 1), (given, 2),
        (rs_third, 3), (rs_sent, 3), (given, 3),
    ):
        if ch < nc:
            step(ch)


def finish(out_in, pg_in, dq, dk, dv, gk, gv, gk_ref, gv_ref, sem):
    copies = []
    for n, dst in enumerate((dq, dk, dv)):
        for part in range(4):
            rows = pl.ds(part * 32, 32)
            copies.append(pltpu.make_async_copy(out_in.at[n, rows], dst.at[rows], sem.at[n, part]))
    for copy in copies:
        copy.start()
    both = jnp.concatenate([pg_in[0].astype(F32), pg_in[1].astype(F32)], axis=1)
    gk_ref[...] = both[:8].astype(BF16)
    gv_ref[...] = both[8:].astype(BF16)
    for n, (src, dst) in enumerate(((gk_ref, gk), (gv_ref, gv))):
        copies.append(pltpu.make_async_copy(src, dst, sem.at[3, n]))
        copies[-1].start()
    for copy in copies:
        copy.wait()


def per_device(queries, keys, values, cotangent, lengths, prompt_keys, prompt_values):
    slots, width = queries.shape
    heads = width // HD // 2
    wide = heads * HD
    cuts = chunks_of(heads)
    nc = len(cuts) - 1
    anywhere = pl.BlockSpec(memory_space=pl.ANY)
    vmem = pl.BlockSpec(memory_space=pltpu.VMEM)
    dma = pltpu.SemaphoreType.DMA
    big = jax.ShapeDtypeStruct((slots, width), BF16)
    small = jax.ShapeDtypeStruct((8, width), BF16)
    out, pg = pl.pallas_call(
        functools.partial(kernel, cuts),
        out_shape=(pltpu.VMEM((3, slots, width), BF16), pltpu.VMEM((2, 16, wide), BF16)),
        in_specs=[pl.BlockSpec(memory_space=pltpu.HBM)] * 7,
        out_specs=(vmem,) * 2,
        scratch_shapes=[
            pltpu.SMEM((1, 4), jnp.int32),
            pltpu.VMEM((8, width), BF16),
            pltpu.VMEM((8, width), BF16),
            pltpu.VMEM((2, slots, wide), BF16),
            pltpu.VMEM((2, slots, wide), BF16),
            pltpu.VMEM((384, wide), BF16),
            pltpu.VMEM((2, slots, wide), BF16),
            pltpu.VMEM((CHIPS, 2, 16, wide), BF16),
            pltpu.VMEM((16, wide), BF16),
            pltpu.VMEM((CHIPS, 2, 16, wide), BF16),
            pltpu.VMEM((2, 2, 2, 16, wide), BF16),
            pltpu.VMEM((2, 2, 16, wide), BF16),
            pltpu.VMEM((9, 16, wide), BF16),
            pltpu.VMEM((2, 136, 128), F32),
            pltpu.VMEM((heads, 2, 128, 128), F32),
            pltpu.VMEM((heads, 2, 128, 128), F32),
            pltpu.VMEM((heads, 128, 256), BF16),
            pltpu.VMEM((heads, 8, 256), F32),
            pltpu.VMEM((3, slots, wide), BF16),
            dma((7,)), dma((5,)), dma((5,)), dma((2,)), dma((2, nc)),
            dma((nc,)), dma((nc, 3)), dma((nc,)), dma((nc, 5)), dma((nc,)),
        ],
        compiler_params=pltpu.CompilerParams(
            collective_id=0, has_side_effects=True, vmem_limit_bytes=40 * 1024 * 1024
        ),
    )(*(
        pltpu.with_memory_space_constraint(x, pltpu.HBM)
        for x in (lengths, queries, keys, values, cotangent, prompt_keys, prompt_values)
    ))
    return pl.pallas_call(
        finish,
        out_shape=(big, big, big, small, small),
        in_specs=[anywhere, vmem],
        out_specs=(anywhere,) * 5,
        scratch_shapes=[pltpu.VMEM((8, width), BF16), pltpu.VMEM((8, width), BF16), dma((4, 4))],
        compiler_params=pltpu.CompilerParams(vmem_limit_bytes=8 * 1024 * 1024),
    )(*(pltpu.with_memory_space_constraint(x, pltpu.VMEM) for x in (out, pg)))


def solution(mesh):
    spec = P(("dp", "resp"), None)
    return jax.shard_map(
        per_device, mesh=mesh, in_specs=(spec,) * 7, out_specs=(spec,) * 5, check_vma=False
    )
```

time: 34.6 us -> 32.4 us (0.936)
  Pallas kernels: 33.8 us -> 31.6 us
    pallas_call x1, Pallas kernels: 32.4 us -> 30.2 us  [per_device(): pl.pallas_call(functools.partial(kernel, cuts), out_shape=(pltpu.VMEM((3,...]
where the time goes in v2:
time: 32.4 us; the launch traced here: 32.2 us
  Pallas kernels  31.6 us (98%)
  between operations  0.64 us (2%)
    pallas_call x1, Pallas kernels, per_device(): pl.pallas_call(functools.partial(kernel, cuts), out_shape=(pltpu.VMEM((3,...  30.2 us
    pallas_call x1, Pallas kernels, per_device(): pl.pallas_call(finish, out_shape=(big, big, big, small, small), in_specs=...  1.42 us

profile of v2, /device:TPU:1, one launch (start us, length us, event | category | flops | bytes accessed | tf_op | source)
XLA Modules:
  0.0 32.2 jit_solution(1426705606043704992)
XLA Ops:
  0.6 30.2 %shard_map.110 = (bf16[3,128,2560]{2,1,0:T(8,128)(2,1)S(1)}, bf16[2,16,1280]{2,1,0:T(8,128)(2,1)S(1)}) custom-call(s32[1,4]{1,0:T(1,128)} %len_hbm.1, bf16[128,2560]{1,0:T(8,128)(2,1)} %q_hbm.1, bf16[128,2560]{1,0:T(8,128)(2,1)} %k_hbm.1, bf16[128,2560]{1,0:T(8,128)(2,1)} %v_hbm.1, bf16[128,2560]{1,0:T(8,128)(2,1)} %co_hbm.1, bf16[8,2560]{1,0:T(8,128)(2,1)} %pk_hbm.1, ...), custom_call_target="tpu_custom_call" | custom-call | tf_op jit(solution)/shard_map/pallas_call | solution.py:404
  30.8 1.4 %shard_map.111 = (bf16[128,2560]{1,0:T(8,128)(2,1)}, bf16[128,2560]{1,0:T(8,128)(2,1)}, bf16[128,2560]{1,0:T(8,128)(2,1)}, bf16[8,2560]{1,0:T(8,128)(2,1)}, bf16[8,2560]{1,0:T(8,128)(2,1)}) custom-call(bf16[3,128,2560]{2,1,0:T(8,128)(2,1)S(1)} %get-tuple-element.7.out_in, bf16[2,16,1280]{2,1,0:T(8,128)(2,1)S(1)} %get-tuple-element.8.pg_in), custom_call_target="tpu_custom_call" | custom-call | tf_op jit(solution)/shard_map/pallas_call | solution.py:439

commit v3 on v2

--- a/solution.py
+++ b/solution.py
@@ -29,7 +29,7 @@
 
 def chunks_of(heads):
     if heads == 10:
-        return (0, 2, 5, 8, 10)
+        return (0, 3, 7, 10)
     return tuple(range(0, heads, 2)) + (heads,)
 
 
@@ -66,7 +66,7 @@
 
     def half(ch, way):
         lo, hi = cuts[ch], cuts[ch + 1]
-        cut = lo + (hi - lo + ch % 2) // 2
+        cut = lo + (hi - lo + ch // 2 % 2) // 2
         return pl.ds(lo * HD, (cut - lo) * HD) if way == 1 else pl.ds(cut * HD, (hi - cut) * HD)
 
     key_rows = (pl.ds(0, 128), pl.ds(256, 128))
@@ -353,20 +353,17 @@
         give_back(ch).wait()
 
     for step, ch in (
-        (own_keys_0, 0), (ag_second, 0), (ag_near, 1),
-        (own_keys_0, 1), (ag_second, 1), (ag_near, 2),
-        (own_keys_0, 2), (ag_second, 2), (ag_near, 3),
-        (own_keys_0, 3), (ag_second, 3),
-        (own_keys_1, 0), (own_keys_1, 1), (prompt_keys, 0), (rs_first, 0),
-        (own_keys_1, 2), (prompt_keys, 1), (rs_first, 1),
-        (own_keys_1, 3), (prompt_keys, 2), (rs_first, 2), (rs_second, 0),
-        (prompt_keys, 3), (rs_first, 3), (rs_second, 1),
-        (gradients, 0), (rs_second, 2), (gradients, 1), (rs_second, 3),
-        (gradients, 2), (gradients, 3),
-        (swapped, 0), (swapped, 1), (swapped, 2), (swapped, 3),
-        (rs_third, 0), (rs_third, 1), (rs_third, 2),
-        (rs_sent, 0), (rs_sent, 1), (rs_sent, 2), (given, 0), (given, 1), (given, 2),
-        (rs_third, 3), (rs_sent, 3), (given, 3),
+        (own_keys_0, 0), (own_keys_0, 1), (ag_second, 0), (ag_near, 1),
+        (own_keys_0, 2), (ag_second, 1), (ag_near, 2),
+        (own_keys_1, 0), (ag_second, 2), (own_keys_1, 1), (own_keys_1, 2),
+        (prompt_keys, 0), (rs_first, 0),
+        (prompt_keys, 1), (rs_first, 1),
+        (prompt_keys, 2), (rs_first, 2), (rs_second, 0), (rs_second, 1),
+        (gradients, 0), (rs_second, 2), (gradients, 1), (gradients, 2),
+        (swapped, 0), (swapped, 1), (swapped, 2),
+        (rs_third, 0), (rs_third, 1),
+        (rs_sent, 0), (rs_sent, 1), (given, 0), (given, 1),
+        (rs_third, 2), (rs_sent, 2), (given, 2),
     ):
         if ch < nc:
             step(ch)

time: 32.4 us -> 33.1 us (1.022)
  Pallas kernels: 31.6 us -> 32.3 us
    pallas_call x1, Pallas kernels: 30.2 us -> 30.9 us  [per_device(): pl.pallas_call(functools.partial(kernel, cuts), out_shape=(pltpu.VMEM((3,...]
where the time goes in v3:
time: 33.1 us; the launch traced here: 32.9 us
  Pallas kernels  32.3 us (98%)
  between operations  0.64 us (2%)
    pallas_call x1, Pallas kernels, per_device(): pl.pallas_call(functools.partial(kernel, cuts), out_shape=(pltpu.VMEM((3,...  30.9 us
    pallas_call x1, Pallas kernels, per_device(): pl.pallas_call(finish, out_shape=(big, big, big, small, small), in_specs=...  1.42 us

profile of v3, /device:TPU:1, one launch (start us, length us, event | category | flops | bytes accessed | tf_op | source)
XLA Modules:
  0.0 32.9 jit_solution(14639485420855377580)
XLA Ops:
  0.6 30.9 %shard_map.110 = (bf16[3,128,2560]{2,1,0:T(8,128)(2,1)S(1)}, bf16[2,16,1280]{2,1,0:T(8,128)(2,1)S(1)}) custom-call(s32[1,4]{1,0:T(1,128)} %len_hbm.1, bf16[128,2560]{1,0:T(8,128)(2,1)} %q_hbm.1, bf16[128,2560]{1,0:T(8,128)(2,1)} %k_hbm.1, bf16[128,2560]{1,0:T(8,128)(2,1)} %v_hbm.1, bf16[128,2560]{1,0:T(8,128)(2,1)} %co_hbm.1, bf16[8,2560]{1,0:T(8,128)(2,1)} %pk_hbm.1, ...), custom_call_target="tpu_custom_call" | custom-call | tf_op jit(solution)/shard_map/pallas_call | solution.py:401
  31.5 1.4 %shard_map.111 = (bf16[128,2560]{1,0:T(8,128)(2,1)}, bf16[128,2560]{1,0:T(8,128)(2,1)}, bf16[128,2560]{1,0:T(8,128)(2,1)}, bf16[8,2560]{1,0:T(8,128)(2,1)}, bf16[8,2560]{1,0:T(8,128)(2,1)}) custom-call(bf16[3,128,2560]{2,1,0:T(8,128)(2,1)S(1)} %get-tuple-element.7.out_in, bf16[2,16,1280]{2,1,0:T(8,128)(2,1)S(1)} %get-tuple-element.8.pg_in), custom_call_target="tpu_custom_call" | custom-call | tf_op jit(solution)/shard_map/pallas_call | solution.py:436

commit v4 on v3

--- a/solution.py
+++ b/solution.py
@@ -81,14 +81,16 @@
         pltpu.make_async_copy(v_hbm.at[:, mine], va_ref.at[0], in_sem.at[5]),
         pltpu.make_async_copy(co_hbm.at[:, mine], co_ref.at[0], in_sem.at[6]),
     ]
-    for load in loads:
-        load.start()
+    loads[0].start()
+    loads[1].start()
 
     barrier = pltpu.get_barrier_semaphore()
     partners = [sibling] + [away(o, other) for o in (1, -1, 2, -2) for other in (0, 1)]
     for partner in partners:
         pl.semaphore_signal(barrier, inc=1, device_id={"resp": partner}, device_id_type=MESH)
 
+    for load in loads[2:]:
+        load.start()
     loads[0].wait()
     loads[1].wait()
     own = jnp.concatenate([pk_ref[...].astype(F32), pv_ref[...].astype(F32)], axis=0)
@@ -304,6 +306,8 @@
         for way in (1, -1):
             rs_mid(ch, 4, way).start()
             rs_mid(ch, 3, way).start()
+
+    def rs_beside(ch):
         for way in (1, -1):
             rs_last(ch, 1, way, part_ref.at[SLOT[way]])
         rs_near(ch).start()
@@ -353,12 +357,12 @@
         give_back(ch).wait()
 
     for step, ch in (
-        (own_keys_0, 0), (own_keys_0, 1), (ag_second, 0), (ag_near, 1),
-        (own_keys_0, 2), (ag_second, 1), (ag_near, 2),
-        (own_keys_1, 0), (ag_second, 2), (own_keys_1, 1), (own_keys_1, 2),
-        (prompt_keys, 0), (rs_first, 0),
-        (prompt_keys, 1), (rs_first, 1),
+        (own_keys_0, 0), (ag_second, 0), (ag_near, 1), (ag_second, 1), (ag_near, 2),
+        (own_keys_0, 1), (ag_second, 2), (own_keys_0, 2), (own_keys_1, 0), (own_keys_1, 1),
+        (prompt_keys, 0), (rs_first, 0), (own_keys_1, 2),
+        (prompt_keys, 1), (rs_first, 1), (rs_beside, 0),
         (prompt_keys, 2), (rs_first, 2), (rs_second, 0), (rs_second, 1),
+        (rs_beside, 1), (rs_beside, 2),
         (gradients, 0), (rs_second, 2), (gradients, 1), (gradients, 2),
         (swapped, 0), (swapped, 1), (swapped, 2),
         (rs_third, 0), (rs_third, 1),

time: 33.1 us -> 33 us (level)
  no operation moved by 1% of the time
where the time goes in v4:
time: 33 us; the launch traced here: 32.9 us
  Pallas kernels  32.2 us (98%)
  between operations  0.64 us (2%)
    pallas_call x1, Pallas kernels, per_device(): pl.pallas_call(functools.partial(kernel, cuts), out_shape=(pltpu.VMEM((3,...  30.8 us
    pallas_call x1, Pallas kernels, per_device(): pl.pallas_call(finish, out_shape=(big, big, big, small, small), in_specs=...  1.42 us

profile of v4, /device:TPU:1, one launch (start us, length us, event | category | flops | bytes accessed | tf_op | source)
XLA Modules:
  0.0 32.9 jit_solution(13549410400461609852)
XLA Ops:
  0.6 30.8 %shard_map.110 = (bf16[3,128,2560]{2,1,0:T(8,128)(2,1)S(1)}, bf16[2,16,1280]{2,1,0:T(8,128)(2,1)S(1)}) custom-call(s32[1,4]{1,0:T(1,128)} %len_hbm.1, bf16[128,2560]{1,0:T(8,128)(2,1)} %q_hbm.1, bf16[128,2560]{1,0:T(8,128)(2,1)} %k_hbm.1, bf16[128,2560]{1,0:T(8,128)(2,1)} %v_hbm.1, bf16[128,2560]{1,0:T(8,128)(2,1)} %co_hbm.1, bf16[8,2560]{1,0:T(8,128)(2,1)} %pk_hbm.1, ...), custom_call_target="tpu_custom_call" | custom-call | tf_op jit(solution)/shard_map/pallas_call | solution.py:405
  31.4 1.4 %shard_map.111 = (bf16[128,2560]{1,0:T(8,128)(2,1)}, bf16[128,2560]{1,0:T(8,128)(2,1)}, bf16[128,2560]{1,0:T(8,128)(2,1)}, bf16[8,2560]{1,0:T(8,128)(2,1)}, bf16[8,2560]{1,0:T(8,128)(2,1)}) custom-call(bf16[3,128,2560]{2,1,0:T(8,128)(2,1)S(1)} %get-tuple-element.7.out_in, bf16[2,16,1280]{2,1,0:T(8,128)(2,1)S(1)} %get-tuple-element.8.pg_in), custom_call_target="tpu_custom_call" | custom-call | tf_op jit(solution)/shard_map/pallas_call | solution.py:440

commit v5 on v2

--- a/solution.py
+++ b/solution.py
@@ -81,14 +81,16 @@
         pltpu.make_async_copy(v_hbm.at[:, mine], va_ref.at[0], in_sem.at[5]),
         pltpu.make_async_copy(co_hbm.at[:, mine], co_ref.at[0], in_sem.at[6]),
     ]
-    for load in loads:
-        load.start()
+    loads[0].start()
+    loads[1].start()
 
     barrier = pltpu.get_barrier_semaphore()
     partners = [sibling] + [away(o, other) for o in (1, -1, 2, -2) for other in (0, 1)]
     for partner in partners:
         pl.semaphore_signal(barrier, inc=1, device_id={"resp": partner}, device_id_type=MESH)
 
+    for load in loads[2:]:
+        load.start()
     loads[0].wait()
     loads[1].wait()
     own = jnp.concatenate([pk_ref[...].astype(F32), pv_ref[...].astype(F32)], axis=0)
@@ -102,6 +104,8 @@
         cols = span(ch)
         for way in (1, -1):
             sem = 2 if kind == 1 else 0 if way == 1 else 1
+            if kind == 1 and ch >= 2:
+                sem = 3 if way == 1 else 4
             for other in (0, 1):
                 src = other_ref.at[:, cols] if other else gat_ref.at[0, 0, :, cols]
                 dst = gat_ref.at[SLOT[-way * kind], other, :, cols]
@@ -112,6 +116,14 @@
 
     def ag_near(ch):
         ag_send_own(ch, 1)
+
+    def ag_pass(ch):
+        for way in (1, -1):
+            block = gat_ref.at[SLOT[-way], :, :, span(ch)]
+            remote(block, block, ag_send.at[ch], ag_recv.at[ch, 3 if way == 1 else 4],
+                   sibling).wait_recv()
+            remote(block, gat_ref.at[SLOT[-way * 2], :, :, span(ch)],
+                   ag_send.at[ch], ag_recv.at[ch, 0 if way == 1 else 1], away(way)).start()
 
     def ag_second(ch):
         for way in (1, -1):
@@ -126,7 +138,7 @@
                    ag_send.at[ch], ag_recv.at[ch, 2], away(way)).start()
 
     def ag_third(ch):
-        rest = gat_ref.at[pl.ds(3, 5), :, :, span(ch)]
+        rest = gat_ref.at[pl.ds(3, 5) if ch < 2 else pl.ds(5, 3), :, :, span(ch)]
         remote(rest, rest, ag_send.at[ch], ag_recv.at[ch, 2], sibling).wait_recv()
 
     def ag_sent(ch):
@@ -147,7 +159,10 @@
     ag_far(0)
     ag_near(0)
     for ch in range(1, nc):
-        ag_far(ch)
+        if ch < 2:
+            ag_far(ch)
+        else:
+            ag_near(ch)
     own_block.start()
     for swap in swaps[:4]:
         swap.start()
@@ -280,7 +295,7 @@
         give_back(ch).start()
 
     def end_at(kind, way, other):
-        return 4 * other + 2 * (kind - 1) + (0 if way == 1 else 1)
+        return (5 if kind == 2 else 0) + 2 * other + (0 if way == 1 else 1)
 
     def rs_last(ch, kind, way, src):
         cols = span(ch)
@@ -297,13 +312,15 @@
 
     def rs_near(ch):
         cols = span(ch)
-        return remote(part_ref.at[0, 1, :, cols], end_ref.at[8, :, cols],
+        return remote(part_ref.at[0, 1, :, cols], end_ref.at[4, :, cols],
                       rs_own.at[ch], rs_recv.at[ch, 0], sibling)
 
     def rs_first(ch):
         for way in (1, -1):
             rs_mid(ch, 4, way).start()
             rs_mid(ch, 3, way).start()
+
+    def rs_beside(ch):
         for way in (1, -1):
             rs_last(ch, 1, way, part_ref.at[SLOT[way]])
         rs_near(ch).start()
@@ -321,18 +338,36 @@
                 at = some.start - cols.start
                 total = total[:, at:at + some.size] + mid_ref[w, 1, other, :, some].astype(F32)
                 tx_ref[w, other, :, some] = total.astype(BF16)
-            rs_last(ch, 2, way, tx_ref.at[w])
+            if ch >= 2:
+                rs_last(ch, 2, way, tx_ref.at[w])
+            else:
+                rs_pass_copy(ch, w, way).start()
+
+    def rs_pass_copy(ch, w, way):
+        cols = span(ch)
+        return remote(tx_ref.at[w, :, :, cols], mid_ref.at[w, 2, :, :, cols],
+                      rs_send.at[ch], rs_recv.at[ch, 5 + w], away(way))
+
+    def rs_pass(ch):
+        cols = span(ch)
+        for w, way in enumerate((1, -1)):
+            rs_pass_copy(ch, w, way).wait_recv()
+            for other in (0, 1):
+                total = part_ref[SLOT[way], other, :, cols].astype(F32)
+                total = total + mid_ref[w, 2, other, :, cols].astype(F32)
+                tx_ref[2 + w, other, :, cols] = total.astype(BF16)
+            rs_last(ch, 1, way, tx_ref.at[2 + w])
+        rs_near(ch).start()
 
     def rs_third(ch):
         cols = span(ch)
-        last = end_ref.at[:, :, cols]
+        last = end_ref.at[pl.ds(0, 9 if ch >= 2 else 5), :, cols]
         remote(last, last, rs_send.at[ch], rs_recv.at[ch, 0], sibling).wait_recv()
         same = part_ref[0, 0, :, cols].astype(F32)
-        for n in range(4):
-            same = same + end_ref[n, :, cols].astype(F32)
         other = end_ref[4, :, cols].astype(F32)
-        for n in range(5, 9):
-            other = other + end_ref[n, :, cols].astype(F32)
+        for n in (0, 5) if ch >= 2 else (0,):
+            same = same + end_ref[n, :, cols].astype(F32) + end_ref[n + 1, :, cols].astype(F32)
+            other = other + end_ref[n + 2, :, cols].astype(F32) + end_ref[n + 3, :, cols].astype(F32)
         for at, total in ((core, same), (1 - core, other)):
             total = jnp.concatenate([total[:8] * SCALE, total[8:]], axis=0)
             pg_ref[at, :, cols] = total.astype(BF16)
@@ -353,15 +388,15 @@
         give_back(ch).wait()
 
     for step, ch in (
-        (own_keys_0, 0), (ag_second, 0), (ag_near, 1),
-        (own_keys_0, 1), (ag_second, 1), (ag_near, 2),
-        (own_keys_0, 2), (ag_second, 2), (ag_near, 3),
+        (own_keys_0, 0), (ag_second, 0), (ag_near, 1), (ag_pass, 2),
+        (own_keys_0, 1), (ag_second, 1), (ag_pass, 3),
+        (own_keys_0, 2), (ag_second, 2),
         (own_keys_0, 3), (ag_second, 3),
         (own_keys_1, 0), (own_keys_1, 1), (prompt_keys, 0), (rs_first, 0),
         (own_keys_1, 2), (prompt_keys, 1), (rs_first, 1),
-        (own_keys_1, 3), (prompt_keys, 2), (rs_first, 2), (rs_second, 0),
-        (prompt_keys, 3), (rs_first, 3), (rs_second, 1),
-        (gradients, 0), (rs_second, 2), (gradients, 1), (rs_second, 3),
+        (own_keys_1, 3), (prompt_keys, 2), (rs_first, 2), (rs_beside, 2), (rs_second, 0),
+        (prompt_keys, 3), (rs_first, 3), (rs_beside, 3), (rs_second, 1), (rs_pass, 0),
+        (gradients, 0), (rs_second, 2), (gradients, 1), (rs_second, 3), (rs_pass, 1),
         (gradients, 2), (gradients, 3),
         (swapped, 0), (swapped, 1), (swapped, 2), (swapped, 3),
         (rs_third, 0), (rs_third, 1), (rs_third, 2),
@@ -417,8 +452,8 @@
             pltpu.VMEM((CHIPS, 2, 16, wide), BF16),
             pltpu.VMEM((16, wide), BF16),
             pltpu.VMEM((CHIPS, 2, 16, wide), BF16),
-            pltpu.VMEM((2, 2, 2, 16, wide), BF16),
-            pltpu.VMEM((2, 2, 16, wide), BF16),
+            pltpu.VMEM((2, 3, 2, 16, wide), BF16),
+            pltpu.VMEM((4, 2, 16, wide), BF16),
             pltpu.VMEM((9, 16, wide), BF16),
             pltpu.VMEM((2, 136, 128), F32),
             pltpu.VMEM((heads, 2, 128, 128), F32),
@@ -427,7 +462,7 @@
             pltpu.VMEM((heads, 8, 256), F32),
             pltpu.VMEM((3, slots, wide), BF16),
             dma((7,)), dma((5,)), dma((5,)), dma((2,)), dma((2, nc)),
-            dma((nc,)), dma((nc, 3)), dma((nc,)), dma((nc, 5)), dma((nc,)),
+            dma((nc,)), dma((nc, 5)), dma((nc,)), dma((nc, 7)), dma((nc,)),
         ],
         compiler_params=pltpu.CompilerParams(
             collective_id=0, has_side_effects=True, vmem_limit_bytes=40 * 1024 * 1024

time: 32.4 us -> 34.5 us (1.065)
  Pallas kernels: 31.6 us -> 33.8 us
    pallas_call x1, Pallas kernels: 30.2 us -> 32.3 us  [per_device(): pl.pallas_call(functools.partial(kernel, cuts), out_shape=(pltpu.VMEM((3,...]
where the time goes in v5:
time: 34.5 us; the launch traced here: 34.4 us
  Pallas kernels  33.8 us (98%)
  between operations  0.64 us (2%)
    pallas_call x1, Pallas kernels, per_device(): pl.pallas_call(functools.partial(kernel, cuts), out_shape=(pltpu.VMEM((3,...  32.3 us
    pallas_call x1, Pallas kernels, per_device(): pl.pallas_call(finish, out_shape=(big, big, big, small, small), in_specs=...  1.42 us

profile of v5, /device:TPU:1, one launch (start us, length us, event | category | flops | bytes accessed | tf_op | source)
XLA Modules:
  0.0 34.4 jit_solution(111673165439928826)
XLA Ops:
  0.6 32.3 %shard_map.110 = (bf16[3,128,2560]{2,1,0:T(8,128)(2,1)S(1)}, bf16[2,16,1280]{2,1,0:T(8,128)(2,1)S(1)}) custom-call(s32[1,4]{1,0:T(1,128)} %len_hbm.1, bf16[128,2560]{1,0:T(8,128)(2,1)} %q_hbm.1, bf16[128,2560]{1,0:T(8,128)(2,1)} %k_hbm.1, bf16[128,2560]{1,0:T(8,128)(2,1)} %v_hbm.1, bf16[128,2560]{1,0:T(8,128)(2,1)} %co_hbm.1, bf16[8,2560]{1,0:T(8,128)(2,1)} %pk_hbm.1, ...), custom_call_target="tpu_custom_call" | custom-call | tf_op jit(solution)/shard_map/pallas_call | solution.py:439
  33.0 1.4 %shard_map.111 = (bf16[128,2560]{1,0:T(8,128)(2,1)}, bf16[128,2560]{1,0:T(8,128)(2,1)}, bf16[128,2560]{1,0:T(8,128)(2,1)}, bf16[8,2560]{1,0:T(8,128)(2,1)}, bf16[8,2560]{1,0:T(8,128)(2,1)}) custom-call(bf16[3,128,2560]{2,1,0:T(8,128)(2,1)S(1)} %get-tuple-element.7.out_in, bf16[2,16,1280]{2,1,0:T(8,128)(2,1)S(1)} %get-tuple-element.8.pg_in), custom_call_target="tpu_custom_call" | custom-call | tf_op jit(solution)/shard_map/pallas_call | solution.py:474

commit v6 on v2

--- a/solution.py
+++ b/solution.py
@@ -353,11 +353,11 @@
         give_back(ch).wait()
 
     for step, ch in (
-        (own_keys_0, 0), (ag_second, 0), (ag_near, 1),
-        (own_keys_0, 1), (ag_second, 1), (ag_near, 2),
-        (own_keys_0, 2), (ag_second, 2), (ag_near, 3),
-        (own_keys_0, 3), (ag_second, 3),
-        (own_keys_1, 0), (own_keys_1, 1), (prompt_keys, 0), (rs_first, 0),
+        (own_keys_0, 0), (own_keys_0, 1), (ag_second, 0), (ag_near, 1),
+        (own_keys_0, 2), (ag_second, 1), (ag_near, 2),
+        (own_keys_0, 3), (ag_second, 2), (ag_near, 3),
+        (own_keys_1, 0), (ag_second, 3),
+        (own_keys_1, 1), (prompt_keys, 0), (rs_first, 0),
         (own_keys_1, 2), (prompt_keys, 1), (rs_first, 1),
         (own_keys_1, 3), (prompt_keys, 2), (rs_first, 2), (rs_second, 0),
         (prompt_keys, 3), (rs_first, 3), (rs_second, 1),

time: 32.4 us -> 32.4 us (level)
  no operation moved by 1% of the time
where the time goes in v6:
time: 32.4 us; the launch traced here: 32.2 us
  Pallas kernels  31.6 us (98%)
  between operations  0.64 us (2%)
    pallas_call x1, Pallas kernels, per_device(): pl.pallas_call(functools.partial(kernel, cuts), out_shape=(pltpu.VMEM((3,...  30.2 us
    pallas_call x1, Pallas kernels, per_device(): pl.pallas_call(finish, out_shape=(big, big, big, small, small), in_specs=...  1.42 us

profile of v6, /device:TPU:1, one launch (start us, length us, event | category | flops | bytes accessed | tf_op | source)
XLA Modules:
  0.0 32.2 jit_solution(15679408268390647673)
XLA Ops:
  0.6 30.2 %shard_map.110 = (bf16[3,128,2560]{2,1,0:T(8,128)(2,1)S(1)}, bf16[2,16,1280]{2,1,0:T(8,128)(2,1)S(1)}) custom-call(s32[1,4]{1,0:T(1,128)} %len_hbm.1, bf16[128,2560]{1,0:T(8,128)(2,1)} %q_hbm.1, bf16[128,2560]{1,0:T(8,128)(2,1)} %k_hbm.1, bf16[128,2560]{1,0:T(8,128)(2,1)} %v_hbm.1, bf16[128,2560]{1,0:T(8,128)(2,1)} %co_hbm.1, bf16[8,2560]{1,0:T(8,128)(2,1)} %pk_hbm.1, ...), custom_call_target="tpu_custom_call" | custom-call | tf_op jit(solution)/shard_map/pallas_call | solution.py:404
  30.8 1.4 %shard_map.111 = (bf16[128,2560]{1,0:T(8,128)(2,1)}, bf16[128,2560]{1,0:T(8,128)(2,1)}, bf16[128,2560]{1,0:T(8,128)(2,1)}, bf16[8,2560]{1,0:T(8,128)(2,1)}, bf16[8,2560]{1,0:T(8,128)(2,1)}) custom-call(bf16[3,128,2560]{2,1,0:T(8,128)(2,1)S(1)} %get-tuple-element.7.out_in, bf16[2,16,1280]{2,1,0:T(8,128)(2,1)S(1)} %get-tuple-element.8.pg_in), custom_call_target="tpu_custom_call" | custom-call | tf_op jit(solution)/shard_map/pallas_call | solution.py:439
